TPU v7x, 1024 devices: a whole 8x8x8 slice. The times are simulated.
1024 devices in a mesh: wide: 128 (over y_lo, z, x), narrow: 8 (over y_hi, core).
Axes of the slice: x: 8, y: 8 (y_hi: 4, y_lo: 2; y = y_hi * 2 + y_lo), z: 8, core: 2. Of those that a mesh axis runs over, the one named last changes fastest.
Arguments:
- right_side: float32 [8, 2048, 12, 128], P('narrow', 'wide'), may hold values from -160 to 160
- hop_blocks: bfloat16 [8, 2048, 9, 64, 128], P('narrow', 'wide'), may hold values from -2 to 6
- restriction: float32 [8, 2048, 64, 128], P('narrow', 'wide'), may hold values from -0.25 to 0.25
Outputs:
- solution_field: float32 [8, 2048, 12, 128], P('narrow', 'wide')
- coarse_residual: float32 [8, 512, 12, 128], P(None, 'wide')
All inputs are finite; a program needn't handle non-finite values.
Results may differ from a plain program's by a relative error of at most 0.0053.
Values may be sent and summed in bfloat16 or wider, within the bound.
A program may use at most 32 MiB of HBM per device.

v0:
```python
import jax
import jax.numpy as jnp
from jax import lax
from jax.sharding import PartitionSpec as P

ITERS = 4
YLOC = 2
LY = 16


def from_behind(value, axis, steps):
    count = lax.axis_size(axis)
    pairs = [(source, (source + steps) % count) for source in range(count)]
    return lax.ppermute(value, axis, pairs)


def padded(cells, sides, width):
    for axis, dim in sides:
        count = lax.axis_size(axis)
        head = lax.slice_in_dim(cells, 0, width, axis=dim)
        tail = lax.slice_in_dim(cells, cells.shape[dim] - width, cells.shape[dim], axis=dim)
        cells = jnp.concatenate(
            [
                lax.ppermute(tail, axis, [(i, (i + 1) % count) for i in range(count)]),
                cells,
                lax.ppermute(head, axis, [((i + 1) % count, i) for i in range(count)]),
            ],
            axis=dim,
        )
    return cells


def complex_pair(vector):
    half = vector.shape[-1] // 2
    real_part = vector[..., :half]
    imag_part = vector[..., half:]
    first = jnp.concatenate([real_part, -imag_part], -1)
    second = jnp.concatenate([imag_part, real_part], -1)
    return (first, second)


def plane_shift(block, step):
    return from_behind(block, "wide", step)


def row_shift(block, step):
    return from_behind(block, "wide", step)


def operate(rounded, hop_blocks):
    sites = rounded.shape[1]
    rhs_count = rounded.shape[2]
    width = rounded.shape[3]
    extended = padded(rounded, (("narrow", 0),), 1)
    grid = rounded[0].reshape(YLOC, sites // YLOC, rhs_count, width)
    rows_y = LY // YLOC
    ylabel = lax.axis_index("wide") % rows_y
    lowest = grid[0:1]
    highest = grid[YLOC - 1 : YLOC]
    z_forward = plane_shift(grid, -rows_y)
    z_backward = plane_shift(grid, rows_y)
    fwd_plain = row_shift(lowest, -1)
    fwd_wrap = row_shift(lowest, rows_y - 1)
    back_plain = row_shift(highest, 1)
    back_wrap = row_shift(highest, -(rows_y - 1))
    fwd_row = jnp.where(ylabel == rows_y - 1, fwd_wrap, fwd_plain)
    back_row = jnp.where(ylabel == 0, back_wrap, back_plain)
    y_forward = jnp.concatenate([grid[1:], fwd_row], 0)
    y_backward = jnp.concatenate([back_row, grid[:-1]], 0)
    flat_shape = (sites, rhs_count, width)
    views = [
        grid,
        jnp.roll(grid, -1, 1),
        jnp.roll(grid, 1, 1),
        y_forward,
        y_backward,
        z_forward,
        z_backward,
    ]
    views = [view.reshape(flat_shape) for view in views] + [extended[2], extended[0]]
    stacked = jnp.stack(views)
    first, second = complex_pair(stacked)
    paired = jnp.stack([first, second])
    result = jnp.einsum(
        "sdak,pdsrk->psra", hop_blocks[0], paired, preferred_element_type=jnp.float32
    )
    return jnp.concatenate([result[0], result[1]], -1)[None]


def restrict(vector, restriction):
    sites = vector.shape[1]
    rhs_count = vector.shape[2]
    first, second = complex_pair(vector[0])
    paired = jnp.stack([first, second])
    result = jnp.einsum(
        "sak,psrk->psra",
        restriction[0],
        paired,
        precision=lax.Precision.HIGHEST,
        preferred_element_type=jnp.float32,
    )
    persite = jnp.concatenate([result[0], result[1]], -1)
    grouped = persite.reshape(YLOC, sites // (YLOC * 2), 2, rhs_count, persite.shape[-1])
    return jnp.sum(grouped, axis=(0, 2))[None]


def partials(image, residual):
    half = image.shape[-1] // 2
    inner_re = jnp.sum(image * residual, axis=(0, 1, 3))
    inner_im = jnp.sum(
        image[..., :half] * residual[..., half:] - image[..., half:] * residual[..., :half],
        axis=(0, 1, 3),
    )
    power = jnp.sum(image * image, axis=(0, 1, 3))
    return (inner_re, inner_im, power)


def combine_sums(local):
    return lax.psum((local[0], local[1], local[2]), ("wide", "narrow"))


def coefficients(totals):
    return (totals[0] / totals[2], totals[1] / totals[2])


def cmul(alpha_re, alpha_im, vector):
    half = vector.shape[-1] // 2
    real_part = vector[..., :half]
    imag_part = vector[..., half:]
    are = alpha_re[:, None]
    aim = alpha_im[:, None]
    return jnp.concatenate(
        [are * real_part - aim * imag_part, are * imag_part + aim * real_part], -1
    )


def per_device(right_side, hop_blocks, restriction):
    solution_field = jnp.zeros_like(right_side)
    residual = right_side
    for step in range(ITERS - 1):
        image = operate(residual.astype(jnp.bfloat16), hop_blocks)
        alpha_re, alpha_im = coefficients(combine_sums(partials(image, residual)))
        solution_field = solution_field + cmul(alpha_re, alpha_im, residual)
        residual = residual - cmul(alpha_re, alpha_im, image)
    image = operate(residual.astype(jnp.bfloat16), hop_blocks)
    local = partials(image, residual)
    alpha_re, alpha_im = coefficients(combine_sums(local))
    solution_field = solution_field + cmul(alpha_re, alpha_im, residual)
    residual = residual - cmul(alpha_re, alpha_im, image)
    coarse_residual = lax.all_gather(restrict(residual, restriction), "narrow", axis=0, tiled=True)
    return (solution_field, coarse_residual)


def solution(mesh):
    placed = (
        P("narrow", "wide", None, None),
        P("narrow", "wide", None, None, None),
        P("narrow", "wide", None, None),
    )
    return jax.shard_map(
        per_device,
        mesh=mesh,
        in_specs=placed,
        out_specs=(P("narrow", "wide", None, None), P(None, "wide", None, None)),
        check_vma=False,
    )
```

profile of v0, /device:TPU:1, one launch (start us, length us, event | category | flops | bytes accessed | tf_op | source)
XLA Modules:
  0.0 621.8 jit_solution(15640357285719271093)
XLA Ops:
  0.6 1.1 constant_dynamic-update-slice_fusion.8
  1.8 3.9 collective-permute-start.3
  5.7 19.1 %collective-permute-start.2 = (bf16[1,8,12,128]{3,2,0,1:T(8,128)(2,1)S(1)}, bf16[1,8,12,128]{3,2,0,1:T(8,128)(2,1)S(1)}, u32[]{:S(2)}, u32[]{:S(2)}) collective-permute-start(bf16[1,8,12,128]{3,2,0,1:T(8,128)(2,1)S(1)} %get-tuple-element.117), channel_id=1, source_target_pairs={{0,968},{8,976},{16,984},{24,992},{32,1000},{40,1008},{48,1016},{5... | collective-permute-start | bytes 73736 | tf_op jit(solution)/shard_map/ppermute | solution.py:14
  24.8 3.4 collective-permute-start.1
  28.2 2.1 collective-permute-start
  30.3 1.9 collective-permute-start.5
  32.3 5.5 collective-permute-start.4
  37.8 4.0 collective-permute-start.6
  42.0 4.3 collective-permute-start.7
  46.8 0.8 collective-permute-done.7
  47.8 0.7 maximum_bitcast_fusion
  48.6 0.8 fusion.33
  50.1 114.3 %all-reduce.3 = (f32[12]{0:T(128)S(1)}, f32[12]{0:T(128)S(1)}, f32[12]{0:T(128)S(1)}) all-reduce(f32[12]{0:T(128)S(1)} %subtract_reduce_fusion.3, f32[12]{0:T(128)S(1)} %fusion.40, f32[12]{0:T(128)S(1)} %get-tuple-element.35), channel_id=1, replica_groups=mesh['wide'=128,'narrow'=8] {'wide','narrow'}, use_global_device_ids=true, to_apply=%region_5.6 | all-reduce | flops 36 | bytes 288 | tf_op jit(solution)/shard_map/psum | solution.py:119
  164.8 3.0 collective-permute-start.11
  167.7 4.0 collective-permute-start.10
  171.8 4.4 collective-permute-start.9
  176.2 3.4 collective-permute-start.8
  179.6 1.9 collective-permute-start.13
  181.6 5.5 collective-permute-start.12
  187.1 4.2 collective-permute-start.14
  191.4 3.0 collective-permute-start.15
  196.8 0.8 fusion.18
  198.4 112.1 %all-reduce.2 = (f32[12]{0:T(128)S(1)}, f32[12]{0:T(128)S(1)}, f32[12]{0:T(128)S(1)}) all-reduce(f32[12]{0:T(128)S(1)} %subtract_reduce_fusion.2, f32[12]{0:T(128)S(1)} %fusion.43, f32[12]{0:T(128)S(1)} %get-tuple-element.30), channel_id=1, replica_groups=mesh['wide'=128,'narrow'=8] {'wide','narrow'}, use_global_device_ids=true, to_apply=%region_11.12 | all-reduce | flops 36 | bytes 288 | tf_op jit(solution)/shard_map/psum | solution.py:119
  310.7 1.9 collective-permute-start.19
  312.7 3.1 collective-permute-start.18
  315.8 6.4 %collective-permute-start.17 = (bf16[1,8,12,128]{3,2,0,1:T(8,128)(2,1)S(1)}, bf16[1,8,12,128]{3,2,0,1:T(8,128)(2,1)S(1)}, u32[]{:S(2)}, u32[]{:S(2)}) collective-permute-start(bf16[1,8,12,128]{3,2,0,1:T(8,128)(2,1)S(1)} %get-tuple-element.106), channel_id=1, source_target_pairs={{0,1016},{8,0},{16,8},{24,16},{32,24},{40,32},{48,40},{56,48},{64,... | collective-permute-start | bytes 73736 | tf_op jit(solution)/shard_map/ppermute | solution.py:14
  322.2 3.4 collective-permute-start.16
  325.6 1.9 collective-permute-start.21
  327.6 5.5 collective-permute-start.20
  333.1 4.8 collective-permute-start.22
  338.0 2.8 collective-permute-start.23
  341.0 1.1 collective-permute-done.23
  343.1 0.8 fusion.23
  344.6 112.4 %all-reduce.1 = (f32[12]{0:T(128)S(1)}, f32[12]{0:T(128)S(1)}, f32[12]{0:T(128)S(1)}) all-reduce(f32[12]{0:T(128)S(1)} %subtract_reduce_fusion.1, f32[12]{0:T(128)S(1)} %fusion.44, f32[12]{0:T(128)S(1)} %get-tuple-element.25), channel_id=1, replica_groups=mesh['wide'=128,'narrow'=8] {'wide','narrow'}, use_global_device_ids=true, to_apply=%region_17.18 | all-reduce | flops 36 | bytes 288 | tf_op jit(solution)/shard_map/psum | solution.py:119
  457.3 1.9 collective-permute-start.27
  459.2 3.1 collective-permute-start.26
  462.3 6.4 %collective-permute-start.25 = (bf16[1,8,12,128]{3,2,0,1:T(8,128)(2,1)S(1)}, bf16[1,8,12,128]{3,2,0,1:T(8,128)(2,1)S(1)}, u32[]{:S(2)}, u32[]{:S(2)}) collective-permute-start(bf16[1,8,12,128]{3,2,0,1:T(8,128)(2,1)S(1)} %get-tuple-element.100), channel_id=1, source_target_pairs={{0,1016},{8,0},{16,8},{24,16},{32,24},{40,32},{48,40},{56,48},{64,... | collective-permute-start | bytes 73736 | tf_op jit(solution)/shard_map/ppermute | solution.py:14
  468.7 3.4 collective-permute-start.24
  472.1 1.9 collective-permute-start.29
  474.2 5.5 collective-permute-start.28
  479.6 4.5 collective-permute-start.30
  484.3 2.6 collective-permute-start.31
  487.1 1.1 collective-permute-done.31
  489.2 0.8 fusion.28
  490.8 112.3 %all-reduce = (f32[12]{0:T(128)S(1)}, f32[12]{0:T(128)S(1)}, f32[12]{0:T(128)S(1)}) all-reduce(f32[12]{0:T(128)S(1)} %subtract_reduce_fusion, f32[12]{0:T(128)S(1)} %fusion.45, f32[12]{0:T(128)S(1)} %get-tuple-element.20), channel_id=1, replica_groups=mesh['wide'=128,'narrow'=8] {'wide','narrow'}, use_global_device_ids=true, to_apply=%region_23.24 | all-reduce | flops 36 | bytes 288 | tf_op jit(solution)/shard_map/psum | solution.py:119
  604.6 0.9 convolution_bitcast_fusion
  605.6 15.4 %all-gather = f32[32,12,128]{2,1,0:T(8,128)S(1)} all-gather(f32[4,12,128]{2,1,0:T(8,128)S(1)} %maximum_reduce_fusion), channel_id=2, replica_groups=mesh['wide'=128,'narrow'=8] {'narrow'}, dimensions={0}, use_global_device_ids=true | all-gather | bytes 221184 | tf_op jit(solution)/shard_map/all_gather | solution.py:150
  621.0 0.8 copy.82
  (151 shorter events, 11.0 us)
Async XLA Ops:
  0.6 48.0 %copy-start = (bf16[1,16,9,64,128]{4,3,2,1,0:T(8,128)(2,1)S(1)}, bf16[1,16,9,64,128]{4,3,2,1,0:T(8,128)(2,1)}, u32[]{:S(2)}) copy-start(bf16[1,16,9,64,128]{4,3,2,1,0:T(8,128)(2,1)} %param.4) | copy-start | bytes 7077892
  1.8 30.6 %collective-permute-start.3 = (bf16[1,8,12,128]{3,2,0,1:T(8,128)(2,1)S(1)}, bf16[1,8,12,128]{3,2,0,1:T(8,128)(2,1)S(1)}, u32[]{:S(2)}, u32[]{:S(2)}) collective-permute-start(bf16[1,8,12,128]{3,2,0,1:T(8,128)(2,1)S(1)} %get-tuple-element.117), channel_id=1, source_target_pairs={{0,8},{8,16},{16,24},{24,32},{32,40},{40,48},{48,56},{56,64},{64,7... | collective-permute-start | bytes 73736 | tf_op jit(solution)/shard_map/ppermute | solution.py:14
  5.7 32.1 %collective-permute-start.2 = (bf16[1,8,12,128]{3,2,0,1:T(8,128)(2,1)S(1)}, bf16[1,8,12,128]{3,2,0,1:T(8,128)(2,1)S(1)}, u32[]{:S(2)}, u32[]{:S(2)}) collective-permute-start(bf16[1,8,12,128]{3,2,0,1:T(8,128)(2,1)S(1)} %get-tuple-element.117), channel_id=1, source_target_pairs={{0,968},{8,976},{16,984},{24,992},{32,1000},{40,1008},{48,1016},{5... | collective-permute-start | bytes 73736 | tf_op jit(solution)/shard_map/ppermute | solution.py:14
  24.8 17.1 %collective-permute-start.1 = (bf16[1,8,12,128]{3,2,0,1:T(8,128)(2,1)S(1)}, bf16[1,8,12,128]{3,2,0,1:T(8,128)(2,1)S(1)}, u32[]{:S(2)}, u32[]{:S(2)}) collective-permute-start(bf16[1,8,12,128]{3,2,0,1:T(8,128)(2,1)S(1)} %get-tuple-element.118), channel_id=1, source_target_pairs={{0,1016},{8,0},{16,8},{24,16},{32,24},{40,32},{48,40},{56,48},{64,... | collective-permute-start | bytes 73736 | tf_op jit(solution)/shard_map/ppermute | solution.py:14
  28.2 18.1 %collective-permute-start = (bf16[1,8,12,128]{3,2,0,1:T(8,128)(2,1)S(1)}, bf16[1,8,12,128]{3,2,0,1:T(8,128)(2,1)S(1)}, u32[]{:S(2)}, u32[]{:S(2)}) collective-permute-start(bf16[1,8,12,128]{3,2,0,1:T(8,128)(2,1)S(1)} %get-tuple-element.118), channel_id=1, source_target_pairs={{0,56},{8,64},{16,72},{24,80},{32,88},{40,96},{48,104},{56,112},{6... | collective-permute-start | bytes 73736 | tf_op jit(solution)/shard_map/ppermute | solution.py:14
  30.3 16.1 %collective-permute-start.5 = (bf16[2,8,12,128]{3,2,1,0:T(8,128)(2,1)S(1)}, bf16[2,8,12,128]{3,2,1,0:T(8,128)(2,1)S(1)}, u32[]{:S(2)}, u32[]{:S(2)}) collective-permute-start(bf16[2,8,12,128]{3,2,1,0:T(8,128)(2,1)S(1)} %bitcast.138), channel_id=1, source_target_pairs={{0,64},{8,72},{16,80},{24,88},{32,96},{40,104},{48,112},{56,120},{... | collective-permute-start | bytes 147464 | tf_op jit(solution)/shard_map/ppermute | solution.py:14
  32.3 14.1 %collective-permute-start.4 = (bf16[2,8,12,128]{3,2,1,0:T(8,128)(2,1)S(1)}, bf16[2,8,12,128]{3,2,1,0:T(8,128)(2,1)S(1)}, u32[]{:S(2)}, u32[]{:S(2)}) collective-permute-start(bf16[2,8,12,128]{3,2,1,0:T(8,128)(2,1)S(1)} %bitcast.141), channel_id=1, source_target_pairs={{0,960},{8,968},{16,976},{24,984},{32,992},{40,1000},{48,1008},{56... | collective-permute-start | bytes 147464 | tf_op jit(solution)/shard_map/ppermute | solution.py:14
  37.8 8.9 %collective-permute-start.6 = (bf16[1,16,12,128]{3,2,0,1:T(8,128)(2,1)S(1)}, bf16[1,16,12,128]{3,2,0,1:T(8,128)(2,1)S(1)}, u32[]{:S(2)}, u32[]{:S(2)}) collective-permute-start(bf16[1,16,12,128]{3,2,0,1:T(8,128)(2,1)S(1)} %get-tuple-element.38), channel_id=1, source_target_pairs={{1,0},{2,1},{3,2},{4,3},{5,4},{6,5},{7,6},{0,7},{9,8},{10,9},{11,1... | collective-permute-start | bytes 147464 | tf_op jit(solution)/shard_map/ppermute | solution.py:26
  42.0 5.6 collective-permute-start.7
  48.6 1.1 copy-start.1
  164.8 16.9 %collective-permute-start.11 = (bf16[1,8,12,128]{3,2,0,1:T(8,128)(2,1)S(1)}, bf16[1,8,12,128]{3,2,0,1:T(8,128)(2,1)S(1)}, u32[]{:S(2)}, u32[]{:S(2)}) collective-permute-start(bf16[1,8,12,128]{3,2,0,1:T(8,128)(2,1)S(1)} %get-tuple-element.111), channel_id=1, source_target_pairs={{0,8},{8,16},{16,24},{24,32},{32,40},{40,48},{48,56},{56,64},{64,7... | collective-permute-start | bytes 73736 | tf_op jit(solution)/shard_map/ppermute | solution.py:14
  167.7 19.4 %collective-permute-start.10 = (bf16[1,8,12,128]{3,2,0,1:T(8,128)(2,1)S(1)}, bf16[1,8,12,128]{3,2,0,1:T(8,128)(2,1)S(1)}, u32[]{:S(2)}, u32[]{:S(2)}) collective-permute-start(bf16[1,8,12,128]{3,2,0,1:T(8,128)(2,1)S(1)} %get-tuple-element.111), channel_id=1, source_target_pairs={{0,968},{8,976},{16,984},{24,992},{32,1000},{40,1008},{48,1016},{5... | collective-permute-start | bytes 73736 | tf_op jit(solution)/shard_map/ppermute | solution.py:14
  171.8 19.7 %collective-permute-start.9 = (bf16[1,8,12,128]{3,2,0,1:T(8,128)(2,1)S(1)}, bf16[1,8,12,128]{3,2,0,1:T(8,128)(2,1)S(1)}, u32[]{:S(2)}, u32[]{:S(2)}) collective-permute-start(bf16[1,8,12,128]{3,2,0,1:T(8,128)(2,1)S(1)} %get-tuple-element.112), channel_id=1, source_target_pairs={{0,1016},{8,0},{16,8},{24,16},{32,24},{40,32},{48,40},{56,48},{64,... | collective-permute-start | bytes 73736 | tf_op jit(solution)/shard_map/ppermute | solution.py:14
  176.2 18.3 %collective-permute-start.8 = (bf16[1,8,12,128]{3,2,0,1:T(8,128)(2,1)S(1)}, bf16[1,8,12,128]{3,2,0,1:T(8,128)(2,1)S(1)}, u32[]{:S(2)}, u32[]{:S(2)}) collective-permute-start(bf16[1,8,12,128]{3,2,0,1:T(8,128)(2,1)S(1)} %get-tuple-element.112), channel_id=1, source_target_pairs={{0,56},{8,64},{16,72},{24,80},{32,88},{40,96},{48,104},{56,112},{6... | collective-permute-start | bytes 73736 | tf_op jit(solution)/shard_map/ppermute | solution.py:14
  179.6 15.1 %collective-permute-start.13 = (bf16[2,8,12,128]{3,2,1,0:T(8,128)(2,1)S(1)}, bf16[2,8,12,128]{3,2,1,0:T(8,128)(2,1)S(1)}, u32[]{:S(2)}, u32[]{:S(2)}) collective-permute-start(bf16[2,8,12,128]{3,2,1,0:T(8,128)(2,1)S(1)} %bitcast.151), channel_id=1, source_target_pairs={{0,64},{8,72},{16,80},{24,88},{32,96},{40,104},{48,112},{56,120},{... | collective-permute-start | bytes 147464 | tf_op jit(solution)/shard_map/ppermute | solution.py:14
  181.6 13.0 %collective-permute-start.12 = (bf16[2,8,12,128]{3,2,1,0:T(8,128)(2,1)S(1)}, bf16[2,8,12,128]{3,2,1,0:T(8,128)(2,1)S(1)}, u32[]{:S(2)}, u32[]{:S(2)}) collective-permute-start(bf16[2,8,12,128]{3,2,1,0:T(8,128)(2,1)S(1)} %bitcast.153), channel_id=1, source_target_pairs={{0,960},{8,968},{16,976},{24,984},{32,992},{40,1000},{48,1008},{56... | collective-permute-start | bytes 147464 | tf_op jit(solution)/shard_map/ppermute | solution.py:14
  187.1 8.0 %collective-permute-start.14 = (bf16[1,16,12,128]{3,2,0,1:T(8,128)(2,1)S(1)}, bf16[1,16,12,128]{3,2,0,1:T(8,128)(2,1)S(1)}, u32[]{:S(2)}, u32[]{:S(2)}) collective-permute-start(bf16[1,16,12,128]{3,2,0,1:T(8,128)(2,1)S(1)} %get-tuple-element.33), channel_id=1, source_target_pairs={{1,0},{2,1},{3,2},{4,3},{5,4},{6,5},{7,6},{0,7},{9,8},{10,9},{11,1... | collective-permute-start | bytes 147464 | tf_op jit(solution)/shard_map/ppermute | solution.py:26
  191.4 4.4 collective-permute-start.15
  310.7 16.9 %collective-permute-start.19 = (bf16[1,8,12,128]{3,2,0,1:T(8,128)(2,1)S(1)}, bf16[1,8,12,128]{3,2,0,1:T(8,128)(2,1)S(1)}, u32[]{:S(2)}, u32[]{:S(2)}) collective-permute-start(bf16[1,8,12,128]{3,2,0,1:T(8,128)(2,1)S(1)} %get-tuple-element.105), channel_id=1, source_target_pairs={{0,8},{8,16},{16,24},{24,32},{32,40},{40,48},{48,56},{56,64},{64,7... | collective-permute-start | bytes 73736 | tf_op jit(solution)/shard_map/ppermute | solution.py:14
  312.7 20.4 %collective-permute-start.18 = (bf16[1,8,12,128]{3,2,0,1:T(8,128)(2,1)S(1)}, bf16[1,8,12,128]{3,2,0,1:T(8,128)(2,1)S(1)}, u32[]{:S(2)}, u32[]{:S(2)}) collective-permute-start(bf16[1,8,12,128]{3,2,0,1:T(8,128)(2,1)S(1)} %get-tuple-element.105), channel_id=1, source_target_pairs={{0,968},{8,976},{16,984},{24,992},{32,1000},{40,1008},{48,1016},{5... | collective-permute-start | bytes 73736 | tf_op jit(solution)/shard_map/ppermute | solution.py:14
  315.8 22.1 %collective-permute-start.17 = (bf16[1,8,12,128]{3,2,0,1:T(8,128)(2,1)S(1)}, bf16[1,8,12,128]{3,2,0,1:T(8,128)(2,1)S(1)}, u32[]{:S(2)}, u32[]{:S(2)}) collective-permute-start(bf16[1,8,12,128]{3,2,0,1:T(8,128)(2,1)S(1)} %get-tuple-element.106), channel_id=1, source_target_pairs={{0,1016},{8,0},{16,8},{24,16},{32,24},{40,32},{48,40},{56,48},{64,... | collective-permute-start | bytes 73736 | tf_op jit(solution)/shard_map/ppermute | solution.py:14
  322.2 18.6 %collective-permute-start.16 = (bf16[1,8,12,128]{3,2,0,1:T(8,128)(2,1)S(1)}, bf16[1,8,12,128]{3,2,0,1:T(8,128)(2,1)S(1)}, u32[]{:S(2)}, u32[]{:S(2)}) collective-permute-start(bf16[1,8,12,128]{3,2,0,1:T(8,128)(2,1)S(1)} %get-tuple-element.106), channel_id=1, source_target_pairs={{0,56},{8,64},{16,72},{24,80},{32,88},{40,96},{48,104},{56,112},{6... | collective-permute-start | bytes 73736 | tf_op jit(solution)/shard_map/ppermute | solution.py:14
  325.6 15.3 %collective-permute-start.21 = (bf16[2,8,12,128]{3,2,1,0:T(8,128)(2,1)S(1)}, bf16[2,8,12,128]{3,2,1,0:T(8,128)(2,1)S(1)}, u32[]{:S(2)}, u32[]{:S(2)}) collective-permute-start(bf16[2,8,12,128]{3,2,1,0:T(8,128)(2,1)S(1)} %bitcast.147), channel_id=1, source_target_pairs={{0,64},{8,72},{16,80},{24,88},{32,96},{40,104},{48,112},{56,120},{... | collective-permute-start | bytes 147464 | tf_op jit(solution)/shard_map/ppermute | solution.py:14
  327.6 13.3 %collective-permute-start.20 = (bf16[2,8,12,128]{3,2,1,0:T(8,128)(2,1)S(1)}, bf16[2,8,12,128]{3,2,1,0:T(8,128)(2,1)S(1)}, u32[]{:S(2)}, u32[]{:S(2)}) collective-permute-start(bf16[2,8,12,128]{3,2,1,0:T(8,128)(2,1)S(1)} %bitcast.149), channel_id=1, source_target_pairs={{0,960},{8,968},{16,976},{24,984},{32,992},{40,1000},{48,1008},{56... | collective-permute-start | bytes 147464 | tf_op jit(solution)/shard_map/ppermute | solution.py:14
  333.1 7.8 %collective-permute-start.22 = (bf16[1,16,12,128]{3,2,0,1:T(8,128)(2,1)S(1)}, bf16[1,16,12,128]{3,2,0,1:T(8,128)(2,1)S(1)}, u32[]{:S(2)}, u32[]{:S(2)}) collective-permute-start(bf16[1,16,12,128]{3,2,0,1:T(8,128)(2,1)S(1)} %get-tuple-element.28), channel_id=1, source_target_pairs={{1,0},{2,1},{3,2},{4,3},{5,4},{6,5},{7,6},{0,7},{9,8},{10,9},{11,1... | collective-permute-start | bytes 147464 | tf_op jit(solution)/shard_map/ppermute | solution.py:26
  338.0 4.1 collective-permute-start.23
  457.3 16.9 %collective-permute-start.27 = (bf16[1,8,12,128]{3,2,0,1:T(8,128)(2,1)S(1)}, bf16[1,8,12,128]{3,2,0,1:T(8,128)(2,1)S(1)}, u32[]{:S(2)}, u32[]{:S(2)}) collective-permute-start(bf16[1,8,12,128]{3,2,0,1:T(8,128)(2,1)S(1)} %get-tuple-element.99), channel_id=1, source_target_pairs={{0,8},{8,16},{16,24},{24,32},{32,40},{40,48},{48,56},{56,64},{64,7... | collective-permute-start | bytes 73736 | tf_op jit(solution)/shard_map/ppermute | solution.py:14
  459.2 20.4 %collective-permute-start.26 = (bf16[1,8,12,128]{3,2,0,1:T(8,128)(2,1)S(1)}, bf16[1,8,12,128]{3,2,0,1:T(8,128)(2,1)S(1)}, u32[]{:S(2)}, u32[]{:S(2)}) collective-permute-start(bf16[1,8,12,128]{3,2,0,1:T(8,128)(2,1)S(1)} %get-tuple-element.99), channel_id=1, source_target_pairs={{0,968},{8,976},{16,984},{24,992},{32,1000},{40,1008},{48,1016},{5... | collective-permute-start | bytes 73736 | tf_op jit(solution)/shard_map/ppermute | solution.py:14
  462.3 21.9 %collective-permute-start.25 = (bf16[1,8,12,128]{3,2,0,1:T(8,128)(2,1)S(1)}, bf16[1,8,12,128]{3,2,0,1:T(8,128)(2,1)S(1)}, u32[]{:S(2)}, u32[]{:S(2)}) collective-permute-start(bf16[1,8,12,128]{3,2,0,1:T(8,128)(2,1)S(1)} %get-tuple-element.100), channel_id=1, source_target_pairs={{0,1016},{8,0},{16,8},{24,16},{32,24},{40,32},{48,40},{56,48},{64,... | collective-permute-start | bytes 73736 | tf_op jit(solution)/shard_map/ppermute | solution.py:14
  468.7 18.2 %collective-permute-start.24 = (bf16[1,8,12,128]{3,2,0,1:T(8,128)(2,1)S(1)}, bf16[1,8,12,128]{3,2,0,1:T(8,128)(2,1)S(1)}, u32[]{:S(2)}, u32[]{:S(2)}) collective-permute-start(bf16[1,8,12,128]{3,2,0,1:T(8,128)(2,1)S(1)} %get-tuple-element.100), channel_id=1, source_target_pairs={{0,56},{8,64},{16,72},{24,80},{32,88},{40,96},{48,104},{56,112},{6... | collective-permute-start | bytes 73736 | tf_op jit(solution)/shard_map/ppermute | solution.py:14
  472.1 15.0 %collective-permute-start.29 = (bf16[2,8,12,128]{3,2,1,0:T(8,128)(2,1)S(1)}, bf16[2,8,12,128]{3,2,1,0:T(8,128)(2,1)S(1)}, u32[]{:S(2)}, u32[]{:S(2)}) collective-permute-start(bf16[2,8,12,128]{3,2,1,0:T(8,128)(2,1)S(1)} %bitcast.143), channel_id=1, source_target_pairs={{0,64},{8,72},{16,80},{24,88},{32,96},{40,104},{48,112},{56,120},{... | collective-permute-start | bytes 147464 | tf_op jit(solution)/shard_map/ppermute | solution.py:14
  474.2 12.9 %collective-permute-start.28 = (bf16[2,8,12,128]{3,2,1,0:T(8,128)(2,1)S(1)}, bf16[2,8,12,128]{3,2,1,0:T(8,128)(2,1)S(1)}, u32[]{:S(2)}, u32[]{:S(2)}) collective-permute-start(bf16[2,8,12,128]{3,2,1,0:T(8,128)(2,1)S(1)} %bitcast.145), channel_id=1, source_target_pairs={{0,960},{8,968},{16,976},{24,984},{32,992},{40,1000},{48,1008},{56... | collective-permute-start | bytes 147464 | tf_op jit(solution)/shard_map/ppermute | solution.py:14
  479.6 7.4 %collective-permute-start.30 = (bf16[1,16,12,128]{3,2,0,1:T(8,128)(2,1)S(1)}, bf16[1,16,12,128]{3,2,0,1:T(8,128)(2,1)S(1)}, u32[]{:S(2)}, u32[]{:S(2)}) collective-permute-start(bf16[1,16,12,128]{3,2,0,1:T(8,128)(2,1)S(1)} %get-tuple-element.23), channel_id=1, source_target_pairs={{1,0},{2,1},{3,2},{4,3},{5,4},{6,5},{7,6},{0,7},{9,8},{10,9},{11,1... | collective-permute-start | bytes 147464 | tf_op jit(solution)/shard_map/ppermute | solution.py:26
  484.3 3.9 collective-permute-start.31
  603.5 1.1 copy-start.2
where the time goes:
time: 623 us; the launch traced here: 622 us
  blocking collectives  467 us (75%)
  starting transfers between devices  133 us (21%)
  other arithmetic  8.59 us (1%)
    psum x4, blocking collectives, combine_sums(): return lax.psum((local[0], local[1], local[2]), ('wide', 'narrow'))  451 us
    ppermute x24, starting transfers between devices, from_behind(): return lax.ppermute(value, axis, pairs)  102 us
    ppermute x4, starting transfers between devices, padded(): lax.ppermute(head, axis, [((i + 1) % count, i) for i in range(count)])  17.6 us
    all_gather x1, blocking collectives, per_device(): lax.all_gather(restrict(residual, restriction), 'narrow', axis=0, tiled=T...  15.4 us
    ppermute x4, starting transfers between devices, padded(): lax.ppermute(tail, axis, [(i, (i + 1) % count) for i in range(count)])  12.8 us
  transfers between devices with their start and end apart: 32, of which 6 were waited for; matrix products, arithmetic and copies ran while one was open for 0% of the time, Pallas kernels for 0%

commit v1 on v0

v1 whole, which is shorter than its diff:
```python
import jax
import jax.numpy as jnp
from jax import lax
from jax.experimental import pallas as pl
from jax.experimental.pallas import tpu as pltpu
from jax.sharding import PartitionSpec as P

F32, BF16 = jnp.float32, jnp.bfloat16
MESH = pl.DeviceIdType.MESH
ITERS = 4
RHS = 12
SITES = 16
HALF = 64
ROWS = SITES * RHS
SLAB = ROWS // 2
PACK = 4 * RHS
SCALE = 1.0 / 16.0


def dot(lhs, rhs):
    return lax.dot_general(lhs, rhs, (((1,), (1,)), ((), ())), preferred_element_type=F32)


def split(value):
    high = value.astype(BF16)
    return high, (value - high.astype(F32)).astype(BF16)


def paired(rows):
    lane = lax.broadcasted_iota(jnp.int32, rows.shape, 1)
    sign = jnp.where(lane < HALF, 1.0, -1.0).astype(rows.dtype)
    return jnp.concatenate([rows * sign, pltpu.roll(rows, HALF, 1)], 0)


def unpack(first, second):
    first = jnp.concatenate([first[0:24, 0:128], first[24:48, 128:256]], 0)
    second = jnp.concatenate([second[0:24, 0:128], second[24:48, 128:256]], 0)
    row = lax.broadcasted_iota(jnp.int32, (PACK, 128), 0)
    lane = lax.broadcasted_iota(jnp.int32, (PACK, 128), 1)
    even = (row < 12) | ((row >= 24) & (row < 36))
    moved = pltpu.roll(jnp.where(even, second, first), HALF, 1)
    return jnp.where(even == (lane < HALF), jnp.where(even, first, second), moved)


def body(
    right_ref, hop_ref, rest_ref, x_ref, coarse_ref,
    rin, hop, rest, vecs, sent, local, big, rows, acc, grams, message, slots0, slots1, slots2, wide_msg,
    rest_hi, rest_lo, mine, xout,
    load_sem, send_sem, recv_sem, red_send, red_recv, gat_send, gat_recv, out_sem,
):
    w = lax.axis_index("wide")
    n = lax.axis_index("narrow")
    ylat, zlat = w % 8, w // 8
    px, pz, plo = w % 8, (w // 8) % 8, w // 64
    phi, pc = n // 2, n % 2
    py = phi * 2 + plo

    load_right = pltpu.make_async_copy(right_ref, rin, load_sem.at[0])
    load_right.start()
    load_hop = pltpu.make_async_copy(hop_ref, hop, load_sem.at[1])
    load_hop.start()
    load_rest = pltpu.make_async_copy(rest_ref, rest, load_sem.at[2])
    load_rest.start()

    z_up, z_down = (((zlat + 1) % 16) * 8 + ylat, n), (((zlat + 15) % 16) * 8 + ylat, n)
    y_up, y_down = (zlat * 8 + (ylat + 1) % 8, n), (zlat * 8 + (ylat + 7) % 8, n)
    t_up, t_down = (w, (n + 1) % 8), (w, (n + 7) % 8)

    def at_x(dx, dc):
        return ((w // 8) * 8 + (px + dx) % 8, phi * 2 + (pc + dc) % 2)

    def at_z(dz):
        return (plo * 64 + ((pz + dz) % 8) * 8 + px, n)

    def at_y(dy):
        other = (py + dy) % 8
        return ((other % 2) * 64 + pz * 8 + px, (other // 2) * 2 + pc)

    phase0 = [at_x(dx, dc) for dx in range(8) for dc in range(2) if dx or dc]
    phase1 = [at_z(dz) for dz in range(1, 8)]
    phase2 = [at_y(dy) for dy in range(1, 8)]

    greeted = [z_up, z_down, t_up, t_down] + phase0 + phase1 + phase2
    barrier = pltpu.get_barrier_semaphore()
    for device in greeted:
        pl.semaphore_signal(barrier, inc=1, device_id=device, device_id_type=MESH)

    load_right.wait()
    for site in range(SITES):
        vecs[0, pl.ds(RHS * site, RHS), :] = rin[pl.ds(site, RHS, stride=SITES), :]

    def halves(i):
        for y in range(2):
            value = vecs[i, pl.ds(SLAB * y, SLAB), :]
            high, low = split(value)
            sent[i, y, 0], sent[i, y, 1] = high, low
            for at, shift in ((0, SLAB - RHS), (1, RHS)):
                moved = pltpu.roll(value, shift, 0)
                high, low = split(moved)
                local[at, y, 0], local[at, y, 1] = high, low

    def halo(i):
        plans = [
            (sent.at[i], big.at[i, 0], z_down),
            (sent.at[i], big.at[i, 1], z_up),
            (sent.at[i], big.at[i, 2], t_down),
            (sent.at[i], big.at[i, 3], t_up),
            (sent.at[i, 0], rows.at[i, 1], y_down),
            (sent.at[i, 1], rows.at[i, 0], y_up),
        ]
        return [
            pltpu.make_async_remote_copy(
                src_ref=src, dst_ref=dst, send_sem=send_sem.at[i, k], recv_sem=recv_sem.at[i, k],
                device_id=device, device_id_type=MESH,
            )
            for k, (src, dst, device) in enumerate(plans)
        ]

    def gram(i):
        lane = lax.broadcasted_iota(jnp.int32, (24, 128), 1)
        sign = jnp.where(lane < HALF, 1.0, -1.0)

        def one(j, total):
            left = vecs[i].reshape(8, 24, 128)
            right = vecs[j].reshape(8, 24, 128)
            turned = pltpu.roll(vecs[j], HALF, 1).reshape(8, 24, 128)
            real = jnp.sum(jnp.sum(left * right, 0), 1, keepdims=True)
            imag = jnp.sum(jnp.sum(left * turned, 0) * sign, 1, keepdims=True)
            entry = i * (i + 1) // 2 + j
            return total + jnp.where(lane == entry, real, 0.0) + jnp.where(lane == entry + 16, imag, 0.0)

        grams[...] = lax.fori_loop(0, i + 1, one, grams[...])

    def weights(y, h, directions):
        first = 8 * y + 4 * h
        return jnp.concatenate([hop[pl.ds(first, 4), d].reshape(256, 128) for d in directions], 1)

    def fields(views, h):
        at = pl.ds(PACK * h, PACK)
        return jnp.concatenate([paired(jnp.concatenate([v[0, at, :], v[1, at, :]], 0)) for v in views], 1)

    groups = [(y, h) for y in range(2) for h in range(2)]

    def early(i):
        for g, (y, h) in enumerate(groups):
            views = [sent.at[i, y], local.at[0, y], local.at[1, y], sent.at[i, 1 - y]]
            acc[g] = dot(fields(views, h), weights(y, h, [0, 1, 2, 3 + y]))

    def late(i):
        for g, (y, h) in enumerate(groups):
            views = [rows.at[i, y]] + [big.at[i, k, y] for k in range(4)]
            total = acc[g] + dot(fields(views, h), weights(y, h, [4 - y, 5, 6, 7, 8]))
            first = total[0:48] + total[48:96]
            second = total[96:144] + total[144:192]
            vecs[i + 1, pl.ds(SLAB * y + PACK * h, PACK), :] = unpack(first, second) * SCALE

    grams[...] = jnp.zeros((24, 128), F32)
    pl.semaphore_wait(barrier, len(greeted))

    def iteration(i, carry):
        halves(i)
        copies = halo(i)
        for copy in copies:
            copy.start()

        @pl.when(i == 0)
        def _():
            load_hop.wait()

        early(i)
        gram(i)
        for copy in copies:
            copy.wait_recv()
        late(i)
        for copy in copies:
            copy.wait_send()
        return carry

    lax.fori_loop(0, ITERS, iteration, 0)
    gram(ITERS)

    both = grams[...] + pltpu.roll(grams[...], RHS, 0)
    packed = both[0:8] + pltpu.roll(both[8:16], 32, 1) + pltpu.roll(both[16:24], 64, 1)
    message[0] = packed[0:4]

    def reduce_over(phase, partners, slots):
        copies = [
            pltpu.make_async_remote_copy(
                src_ref=message.at[phase], dst_ref=slots.at[k],
                send_sem=red_send.at[phase], recv_sem=red_recv.at[phase],
                device_id=device, device_id_type=MESH,
            )
            for k, device in enumerate(partners)
        ]
        for copy in copies:
            copy.start()
        return lambda: (
            pltpu.make_async_copy(slots, slots, red_recv.at[phase]).wait(),
            pltpu.make_async_copy(slots, slots, red_send.at[phase]).wait(),
        )

    finish = reduce_over(0, phase0, slots0)
    load_rest.wait()
    for site in range(SITES):
        rest_hi[site], rest_lo[site] = split(rest[site])
    finish()
    message[1] = message[0] + jnp.sum(slots0[...], 0)
    reduce_over(1, phase1, slots1)()
    message[2] = message[1] + jnp.sum(slots1[...], 0)
    reduce_over(2, phase2, slots2)()
    total = message[2] + jnp.sum(slots2[...], 0)
    wide_msg[0:4, :] = total
    wide_msg[4:8, :] = total
    table = wide_msg[...]

    def entry(e):
        return pltpu.roll(table, (128 - e) % 128, 1)

    g = {}
    for i in range(5):
        for j in range(i + 1):
            e = i * (i + 1) // 2 + j
            g[i, j] = (entry(e), entry(16 + e) if i != j else jnp.zeros((8, 128), F32))

    def times(a, b):
        return a[0] * b[0] - a[1] * b[1], a[0] * b[1] + a[1] * b[0]

    def minus(a, b):
        return a[0] - b[0], a[1] - b[1]

    alphas = []
    for k in range(ITERS):
        inner, power = g[1, 0], g[1, 1][0]
        alpha = (inner[0] / power, inner[1] / power)
        alphas.append(alpha)
        size = alpha[0] * alpha[0] + alpha[1] * alpha[1]
        if k == ITERS - 1:
            break
        top = 4 - k
        later = {}
        for i in range(1, top):
            for j in range(i + 1):
                ahead = g[i, j + 1] if j + 1 <= i else (g[j + 1, i][0], -g[j + 1, i][1])
                value = minus(g[i, j], times(alpha, ahead))
                value = minus(value, times((alpha[0], -alpha[1]), g[i + 1, j]))
                far = g[i + 1, j + 1]
                later[i, j] = (value[0] + size * far[0], value[1] + size * far[1])
        g = later

    one = (jnp.ones((8, 128), F32), jnp.zeros((8, 128), F32))
    residual = [one]
    iterate = []
    for alpha in alphas:
        scaled = (alpha[0] * SCALE, alpha[1] * SCALE)
        added = [times(scaled, c) for c in residual]
        iterate = [
            (a[0] + b[0], a[1] + b[1]) if b is not None else a
            for a, b in zip(added, iterate + [None] * (len(added) - len(iterate)))
        ]
        moved = [times(alpha, c) for c in residual]
        grown = [residual[0]]
        for j in range(1, len(residual)):
            grown.append(minus(residual[j], moved[j - 1]))
        grown.append((-moved[-1][0], -moved[-1][1]))
        residual = grown

    sub = lax.broadcasted_iota(jnp.int32, (8, 128), 0) < 4
    left_half = lax.broadcasted_iota(jnp.int32, (24, 128), 1) < HALF

    def spread(value):
        c0, c1, c2 = (jnp.broadcast_to(value[:, at : at + 1], (8, 128)) for at in (0, 32, 64))
        return jnp.concatenate([jnp.where(sub, c0, c2), jnp.where(sub, c1, c0), jnp.where(sub, c2, c1)], 0)

    def coefficient(pair):
        imag = spread(pair[1])
        return spread(pair[0])[None], jnp.where(left_half, -imag, imag)[None]

    def vector(j):
        return vecs[j].reshape(8, 24, 128), pltpu.roll(vecs[j], HALF, 1).reshape(8, 24, 128)

    last = vecs[0].reshape(8, 24, 128)
    field = jnp.zeros((8, 24, 128), F32)
    for j in range(5):
        plain, turned = vector(j)
        if j > 0:
            re, im = coefficient(residual[j])
            last = last + re * plain + im * turned
        if j < ITERS:
            re, im = coefficient(iterate[j])
            field = field + re * plain + im * turned
    last = last.reshape(ROWS, 128)
    field = field.reshape(ROWS, 128)

    for h in range(2):
        pieces = [split(last[SLAB * y + PACK * h : SLAB * y + PACK * (h + 1)]) for y in range(2)]
        both_rows = jnp.concatenate([paired(jnp.concatenate(p, 0)) for p in pieces], 1)
        high_rows = jnp.concatenate([paired(p[0]) for p in pieces], 1)

        def blocks(ref):
            return jnp.concatenate([ref[8 * y + 4 * h : 8 * y + 4 * h + 4].reshape(256, 128) for y in range(2)], 1)

        main = dot(both_rows, blocks(rest_hi))
        rest_part = dot(high_rows, blocks(rest_lo))
        first = main[0:48] + main[48:96] + rest_part[0:48]
        second = main[96:144] + main[144:192] + rest_part[48:96]
        value = unpack(first, second)
        value = value + pltpu.roll(value, PACK - RHS, 0)
        mine[:, 2 * h, :] = value[0:12]
        mine[:, 2 * h + 1, :] = value[24:36]

    other = (w, phi * 2 + (1 - pc))

    def gather(k, src, slot, device):
        return pltpu.make_async_remote_copy(
            src_ref=src, dst_ref=coarse_ref.at[slot], send_sem=gat_send.at[k], recv_sem=gat_recv.at[k],
            device_id=device, device_id_type=MESH,
        )

    first_hop = [gather(k, mine, n, (w, ((phi + k) % 4) * 2 + pc)) for k in (2, 1, 3)]
    first_hop.append(gather(0, mine, n, other))
    for copy in first_hop:
        copy.start()
    keep = pltpu.make_async_copy(mine, coarse_ref.at[n], out_sem.at[0])
    keep.start()
    for site in range(SITES):
        xout[pl.ds(site, RHS, stride=SITES), :] = field[RHS * site : RHS * (site + 1)]
    put_x = pltpu.make_async_copy(xout, x_ref, out_sem.at[1])
    put_x.start()
    second_hop = []
    for k, copy in zip((2, 1, 3), first_hop):
        copy.wait_recv()
        slot = ((phi + 4 - k) % 4) * 2 + pc
        second_hop.append(gather(4 + k, coarse_ref.at[slot], slot, other))
        second_hop[-1].start()
    first_hop[3].wait_recv()
    for copy in second_hop:
        copy.wait_recv()
    for copy in first_hop + second_hop:
        copy.wait_send()
    keep.wait()
    put_x.wait()


def per_device(right_side, hop_blocks, restriction):
    right = jnp.transpose(right_side[0], (1, 0, 2)).reshape(ROWS, 128)
    x, coarse = pl.pallas_call(
        body,
        out_shape=(jax.ShapeDtypeStruct((ROWS, 128), F32), jax.ShapeDtypeStruct((8, RHS, 4, 128), F32)),
        in_specs=[pl.BlockSpec(memory_space=pl.ANY)] * 3,
        out_specs=(pl.BlockSpec(memory_space=pl.ANY), pl.BlockSpec(memory_space=pltpu.VMEM)),
        scratch_shapes=[
            pltpu.VMEM((ROWS, 128), F32),
            pltpu.VMEM((SITES, 9, 64, 128), BF16),
            pltpu.VMEM((SITES, 64, 128), F32),
            pltpu.VMEM((ITERS + 1, ROWS, 128), F32),
            pltpu.VMEM((ITERS, 2, 2, SLAB, 128), BF16),
            pltpu.VMEM((2, 2, 2, SLAB, 128), BF16),
            pltpu.VMEM((ITERS, 4, 2, 2, SLAB, 128), BF16),
            pltpu.VMEM((ITERS, 2, 2, SLAB, 128), BF16),
            pltpu.VMEM((4, 192, 256), F32),
            pltpu.VMEM((24, 128), F32),
            pltpu.VMEM((3, 4, 128), F32),
            pltpu.VMEM((15, 4, 128), F32),
            pltpu.VMEM((7, 4, 128), F32),
            pltpu.VMEM((7, 4, 128), F32),
            pltpu.VMEM((8, 128), F32),
            pltpu.VMEM((SITES, 64, 128), BF16),
            pltpu.VMEM((SITES, 64, 128), BF16),
            pltpu.VMEM((RHS, 4, 128), F32),
            pltpu.VMEM((ROWS, 128), F32),
            pltpu.SemaphoreType.DMA((3,)),
            pltpu.SemaphoreType.DMA((ITERS, 6)),
            pltpu.SemaphoreType.DMA((ITERS, 6)),
            pltpu.SemaphoreType.DMA((3,)),
            pltpu.SemaphoreType.DMA((3,)),
            pltpu.SemaphoreType.DMA((8,)),
            pltpu.SemaphoreType.DMA((8,)),
            pltpu.SemaphoreType.DMA((2,)),
        ],
        compiler_params=pltpu.CompilerParams(
            collective_id=0, has_side_effects=True, vmem_limit_bytes=56 * 1024 * 1024
        ),
        cost_estimate=pl.CostEstimate(flops=500_000_000, bytes_accessed=4_000_000, transcendentals=0),
        name="smooth",
    )(right, hop_blocks[0], restriction[0])
    x = jnp.transpose(x.reshape(RHS, SITES, 128), (1, 0, 2))[None]
    return x, jnp.transpose(coarse, (0, 2, 1, 3))


def solution(mesh):
    placed = (
        P("narrow", "wide", None, None),
        P("narrow", "wide", None, None, None),
        P("narrow", "wide", None, None),
    )
    return jax.shard_map(
        per_device,
        mesh=mesh,
        in_specs=placed,
        out_specs=(P("narrow", "wide", None, None), P(None, "wide", None, None)),
        check_vma=False,
    )
```

time: 623 us -> 77.3 us (0.12)
  blocking collectives: 467 us -> 0 us
  starting transfers between devices: 133 us -> 0 us
  Pallas kernels: 0 us -> 73.3 us
  other arithmetic: 8.59 us -> 0 us
    psum x4 -> x0, blocking collectives: 451 us -> none  [combine_sums(): return lax.psum((local[0], local[1], local[2]), ('wide', 'narrow'))]
    ppermute x32 -> x0, starting transfers between devices: 133 us -> none  [the longest x24 102 us: from_behind(): return lax.ppermute(value, axis, pairs)]
    pallas_call x0 -> x1, Pallas kernels: none -> 73.3 us  [per_device(): pl.pallas_call(body, out_shape=(jax.ShapeDtypeStruct((ROWS, 128), F32), j...]
    all_gather x1 -> x0, blocking collectives: 15.4 us -> none  [per_device(): lax.all_gather(restrict(residual, restriction), 'narrow', axis=0, tiled=T...]
  transfers between devices with their start and end apart: 32 -> 0, of which waited for: 6 -> 0; matrix products, arithmetic and copies ran while one was open for 0% -> 0% of each run, Pallas kernels for 0% -> 0%
where the time goes in v1:
time: 77.3 us; the launch traced here: 77 us
  Pallas kernels  73.3 us (95%)
  local copies, waits for them, and re-layouts  3.16 us (4%)
    pallas_call x1, Pallas kernels, per_device(): pl.pallas_call(body, out_shape=(jax.ShapeDtypeStruct((ROWS, 128), F32), j...  73.3 us
    unnamed x2, local copies, waits for them, and re-layouts  3.16 us

profile of v1, /device:TPU:1, one launch (start us, length us, event | category | flops | bytes accessed | tf_op | source)
XLA Modules:
  0.0 77.0 jit_solution(640726332958176491)
XLA Ops:
  0.6 73.3 %smooth.1 = (f32[192,128]{1,0:T(8,128)}, f32[8,12,4,128]{3,2,1,0:T(4,128)}) custom-call(f32[192,128]{1,0:T(8,128)} %bitcast.16, bf16[16,9,64,128]{3,2,1,0:T(8,128)(2,1)} %bitcast.13, f32[16,64,128]{2,1,0:T(8,128)} %bitcast.14), custom_call_target="tpu_custom_call" | custom-call | flops 500000000 | bytes 4000000 | tf_op jit(solution)/shard_map/smooth/pallas_call | solution.py:346
  73.9 1.5 %copy.7 = f32[1,16,12,128]{3,1,2,0:T(8,128)} copy(f32[1,16,12,128]{3,1,2,0:T(8,128)} %bitcast.17) | data formatting | bytes 196608
  75.4 1.6 %copy.8 = f32[8,4,12,128]{3,1,2,0:T(4,128)} copy(f32[8,4,12,128]{3,1,2,0:T(4,128)} %bitcast.15) | data formatting | bytes 393216

commit v2 on v1

--- a/solution.py
+++ b/solution.py
@@ -45,7 +45,7 @@
 def body(
     right_ref, hop_ref, rest_ref, x_ref, coarse_ref,
     rin, hop, rest, vecs, sent, local, big, rows, acc, grams, message, slots0, slots1, slots2, wide_msg,
-    rest_hi, rest_lo, mine, xout,
+    rest_hi, rest_lo, mine, posted, xout,
     load_sem, send_sem, recv_sem, red_send, red_recv, gat_send, gat_recv, out_sem,
 ):
     w = lax.axis_index("wide")
@@ -66,21 +66,26 @@
     y_up, y_down = (zlat * 8 + (ylat + 1) % 8, n), (zlat * 8 + (ylat + 7) % 8, n)
     t_up, t_down = (w, (n + 1) % 8), (w, (n + 7) % 8)
 
-    def at_x(dx, dc):
-        return ((w // 8) * 8 + (px + dx) % 8, phi * 2 + (pc + dc) % 2)
-
-    def at_z(dz):
-        return (plo * 64 + ((pz + dz) % 8) * 8 + px, n)
-
-    def at_y(dy):
-        other = (py + dy) % 8
-        return ((other % 2) * 64 + pz * 8 + px, (other // 2) * 2 + pc)
-
-    phase0 = [at_x(dx, dc) for dx in range(8) for dc in range(2) if dx or dc]
-    phase1 = [at_z(dz) for dz in range(1, 8)]
-    phase2 = [at_y(dy) for dy in range(1, 8)]
-
-    greeted = [z_up, z_down, t_up, t_down] + phase0 + phase1 + phase2
+    other = (w, phi * 2 + (1 - pc))
+
+    def at_xy(offset):
+        return ((w // 8) * 8 + (px + offset) % 8, ((phi + offset // 8) % 4) * 2 + pc)
+
+    def at_zy(offset):
+        return (((plo + offset // 8) % 2) * 64 + ((pz + offset) % 8) * 8 + px, n)
+
+    wide_steps = [1 + k + 15 * pc for k in range(16)]
+    deep_steps = [1 + k + 7 * pc for k in range(8)]
+
+    def back_xy(offset):
+        return ((w // 8) * 8 + (px + 64 - offset) % 8, ((phi + 4 - offset // 8) % 4) * 2 + pc)
+
+    def back_zy(offset):
+        return (((plo + 2 - offset // 8) % 2) * 64 + ((pz + 64 - offset) % 8) * 8 + px, n)
+
+    gathered = [(w, ((phi + k) % 4) * 2 + pc) for k in (2, 1, 3)]
+    greeted = [z_up, z_down, t_up, t_down, y_up, y_down, other] + gathered
+    greeted += [back_xy(o) for o in wide_steps] + [back_zy(o) for o in deep_steps]
     barrier = pltpu.get_barrier_semaphore()
     for device in greeted:
         pl.semaphore_signal(barrier, inc=1, device_id=device, device_id_type=MESH)
@@ -89,15 +94,15 @@
     for site in range(SITES):
         vecs[0, pl.ds(RHS * site, RHS), :] = rin[pl.ds(site, RHS, stride=SITES), :]
 
-    def halves(i):
+    def outgoing(i):
+        for y in range(2):
+            sent[i, y, 0], sent[i, y, 1] = split(vecs[i, pl.ds(SLAB * y, SLAB), :])
+
+    def shifted(i):
         for y in range(2):
             value = vecs[i, pl.ds(SLAB * y, SLAB), :]
-            high, low = split(value)
-            sent[i, y, 0], sent[i, y, 1] = high, low
             for at, shift in ((0, SLAB - RHS), (1, RHS)):
-                moved = pltpu.roll(value, shift, 0)
-                high, low = split(moved)
-                local[at, y, 0], local[at, y, 1] = high, low
+                local[at, y, 0], local[at, y, 1] = split(pltpu.roll(value, shift, 0))
 
     def halo(i):
         plans = [
@@ -118,17 +123,22 @@
 
     def gram(i):
         lane = lax.broadcasted_iota(jnp.int32, (24, 128), 1)
-        sign = jnp.where(lane < HALF, 1.0, -1.0)
+        sign = jnp.where(lane < HALF, -1.0, 1.0)[None]
+        left = vecs[i].reshape(8, 24, 128)
+        turned = pltpu.roll(vecs[i], HALF, 1).reshape(8, 24, 128) * sign
 
         def one(j, total):
-            left = vecs[i].reshape(8, 24, 128)
             right = vecs[j].reshape(8, 24, 128)
-            turned = pltpu.roll(vecs[j], HALF, 1).reshape(8, 24, 128)
             real = jnp.sum(jnp.sum(left * right, 0), 1, keepdims=True)
-            imag = jnp.sum(jnp.sum(left * turned, 0) * sign, 1, keepdims=True)
+            imag = jnp.sum(jnp.sum(turned * right, 0), 1, keepdims=True)
             entry = i * (i + 1) // 2 + j
             return total + jnp.where(lane == entry, real, 0.0) + jnp.where(lane == entry + 16, imag, 0.0)
 
+        if isinstance(i, int):
+            total = grams[...]
+            for j in range(i + 1):
+                total = one(j, total)
+            return total
         grams[...] = lax.fori_loop(0, i + 1, one, grams[...])
 
     def weights(y, h, directions):
@@ -146,22 +156,28 @@
             views = [sent.at[i, y], local.at[0, y], local.at[1, y], sent.at[i, 1 - y]]
             acc[g] = dot(fields(views, h), weights(y, h, [0, 1, 2, 3 + y]))
 
+    def middle(i):
+        for g, (y, h) in enumerate(groups):
+            views = [rows.at[i, y], big.at[i, 0, y], big.at[i, 1, y]]
+            acc[g] += dot(fields(views, h), weights(y, h, [4 - y, 5, 6]))
+
     def late(i):
         for g, (y, h) in enumerate(groups):
-            views = [rows.at[i, y]] + [big.at[i, k, y] for k in range(4)]
-            total = acc[g] + dot(fields(views, h), weights(y, h, [4 - y, 5, 6, 7, 8]))
+            views = [big.at[i, 2, y], big.at[i, 3, y]]
+            total = acc[g] + dot(fields(views, h), weights(y, h, [7, 8]))
             first = total[0:48] + total[48:96]
             second = total[96:144] + total[144:192]
             vecs[i + 1, pl.ds(SLAB * y + PACK * h, PACK), :] = unpack(first, second) * SCALE
 
     grams[...] = jnp.zeros((24, 128), F32)
+    outgoing(0)
     pl.semaphore_wait(barrier, len(greeted))
 
     def iteration(i, carry):
-        halves(i)
         copies = halo(i)
         for copy in copies:
             copy.start()
+        shifted(i)
 
         @pl.when(i == 0)
         def _():
@@ -169,17 +185,23 @@
 
         early(i)
         gram(i)
-        for copy in copies:
-            copy.wait_recv()
+        for k in (4, 5, 0, 1):
+            copies[k].wait_recv()
+        middle(i)
+        for k in (2, 3):
+            copies[k].wait_recv()
         late(i)
-        for copy in copies:
-            copy.wait_send()
+
+        @pl.when(i < ITERS - 1)
+        def _():
+            outgoing(i + 1)
+
         return carry
 
     lax.fori_loop(0, ITERS, iteration, 0)
-    gram(ITERS)
-
-    both = grams[...] + pltpu.roll(grams[...], RHS, 0)
+    sums = gram(ITERS)
+
+    both = sums + pltpu.roll(sums, RHS, 0)
     packed = both[0:8] + pltpu.roll(both[8:16], 32, 1) + pltpu.roll(both[16:24], 64, 1)
     message[0] = packed[0:4]
 
@@ -194,21 +216,38 @@
         ]
         for copy in copies:
             copy.start()
-        return lambda: (
-            pltpu.make_async_copy(slots, slots, red_recv.at[phase]).wait(),
-            pltpu.make_async_copy(slots, slots, red_send.at[phase]).wait(),
-        )
-
-    finish = reduce_over(0, phase0, slots0)
+        return [pltpu.make_async_copy(slots, slots, sem.at[phase]) for sem in (red_recv, red_send)]
+
+    def part(own, slots):
+        return jnp.sum(slots[1:], 0) + jnp.where(pc == 0, own + slots[0], 0.0)
+
+    waits = [reduce_over(0, [other], slots0.at[0:1])]
     load_rest.wait()
+    waits[0][0].wait()
+    message[1] = message[0] + slots0[0]
+    waits.append(reduce_over(1, [at_xy(o) for o in wide_steps], slots1))
     for site in range(SITES):
         rest_hi[site], rest_lo[site] = split(rest[site])
-    finish()
-    message[1] = message[0] + jnp.sum(slots0[...], 0)
-    reduce_over(1, phase1, slots1)()
-    message[2] = message[1] + jnp.sum(slots1[...], 0)
-    reduce_over(2, phase2, slots2)()
-    total = message[2] + jnp.sum(slots2[...], 0)
+    waits[1][0].wait()
+    message[2] = part(message[1], slots1[...])
+    waits.append(reduce_over(2, [other], slots0.at[1:2]))
+    waits[2][0].wait()
+    message[3] = message[2] + slots0[1]
+    waits.append(reduce_over(3, [at_zy(o) for o in deep_steps], slots2))
+
+    def drain(i, carry):
+        for copy in halo(i):
+            copy.wait_send()
+        return carry
+
+    lax.fori_loop(0, ITERS, drain, 0)
+    waits[3][0].wait()
+    message[4] = part(message[3], slots2[...])
+    waits.append(reduce_over(4, [other], slots0.at[2:3]))
+    for wait in waits[:4]:
+        wait[1].wait()
+    waits[4][0].wait()
+    total = message[4] + slots0[2]
     wide_msg[0:4, :] = total
     wide_msg[4:8, :] = total
     table = wide_msg[...]
@@ -305,47 +344,50 @@
         second = main[96:144] + main[144:192] + rest_part[48:96]
         value = unpack(first, second)
         value = value + pltpu.roll(value, PACK - RHS, 0)
-        mine[:, 2 * h, :] = value[0:12]
-        mine[:, 2 * h + 1, :] = value[24:36]
-
-    other = (w, phi * 2 + (1 - pc))
-
-    def gather(k, src, slot, device):
+        mine[pl.ds(2 * h, RHS, stride=4), :] = value[0:12]
+        mine[pl.ds(2 * h + 1, RHS, stride=4), :] = value[24:36]
+    posted[n] = mine[...].astype(BF16)
+
+    def gather(k, slot, device):
         return pltpu.make_async_remote_copy(
-            src_ref=src, dst_ref=coarse_ref.at[slot], send_sem=gat_send.at[k], recv_sem=gat_recv.at[k],
+            src_ref=posted.at[slot], dst_ref=posted.at[slot], send_sem=gat_send.at[k], recv_sem=gat_recv.at[k],
             device_id=device, device_id_type=MESH,
         )
 
-    first_hop = [gather(k, mine, n, (w, ((phi + k) % 4) * 2 + pc)) for k in (2, 1, 3)]
-    first_hop.append(gather(0, mine, n, other))
+    first_hop = [gather(k, n, device) for k, device in zip((2, 1, 3), gathered)]
+    first_hop.append(gather(0, n, other))
     for copy in first_hop:
         copy.start()
-    keep = pltpu.make_async_copy(mine, coarse_ref.at[n], out_sem.at[0])
-    keep.start()
     for site in range(SITES):
         xout[pl.ds(site, RHS, stride=SITES), :] = field[RHS * site : RHS * (site + 1)]
-    put_x = pltpu.make_async_copy(xout, x_ref, out_sem.at[1])
+    put_x = pltpu.make_async_copy(xout, x_ref, out_sem.at[0])
     put_x.start()
     second_hop = []
-    for k, copy in zip((2, 1, 3), first_hop):
+    for k, copy in zip((1, 3, 2), (first_hop[1], first_hop[2], first_hop[0])):
         copy.wait_recv()
-        slot = ((phi + 4 - k) % 4) * 2 + pc
-        second_hop.append(gather(4 + k, coarse_ref.at[slot], slot, other))
+        second_hop.append(gather(4 + k, ((phi + 4 - k) % 4) * 2 + pc, other))
         second_hop[-1].start()
     first_hop[3].wait_recv()
     for copy in second_hop:
         copy.wait_recv()
+    coarse_ref[...] = posted[...].astype(F32)
     for copy in first_hop + second_hop:
         copy.wait_send()
-    keep.wait()
+    waits[4][1].wait()
     put_x.wait()
+
+
+def hand_over(x_in, coarse_in, x_out, coarse_out):
+    x_out[...] = x_in[...]
+    coarse_out[...] = coarse_in[...]
 
 
 def per_device(right_side, hop_blocks, restriction):
     right = jnp.transpose(right_side[0], (1, 0, 2)).reshape(ROWS, 128)
-    x, coarse = pl.pallas_call(
+    shapes = (jax.ShapeDtypeStruct((ROWS, 128), F32), jax.ShapeDtypeStruct((8, 4 * RHS, 128), F32))
+    held = pl.pallas_call(
         body,
-        out_shape=(jax.ShapeDtypeStruct((ROWS, 128), F32), jax.ShapeDtypeStruct((8, RHS, 4, 128), F32)),
+        out_shape=shapes,
         in_specs=[pl.BlockSpec(memory_space=pl.ANY)] * 3,
         out_specs=(pl.BlockSpec(memory_space=pl.ANY), pl.BlockSpec(memory_space=pltpu.VMEM)),
         scratch_shapes=[
@@ -359,23 +401,24 @@
             pltpu.VMEM((ITERS, 2, 2, SLAB, 128), BF16),
             pltpu.VMEM((4, 192, 256), F32),
             pltpu.VMEM((24, 128), F32),
+            pltpu.VMEM((5, 4, 128), F32),
             pltpu.VMEM((3, 4, 128), F32),
-            pltpu.VMEM((15, 4, 128), F32),
-            pltpu.VMEM((7, 4, 128), F32),
-            pltpu.VMEM((7, 4, 128), F32),
+            pltpu.VMEM((16, 4, 128), F32),
+            pltpu.VMEM((8, 4, 128), F32),
             pltpu.VMEM((8, 128), F32),
             pltpu.VMEM((SITES, 64, 128), BF16),
             pltpu.VMEM((SITES, 64, 128), BF16),
-            pltpu.VMEM((RHS, 4, 128), F32),
+            pltpu.VMEM((4 * RHS, 128), F32),
+            pltpu.VMEM((8, 4 * RHS, 128), BF16),
             pltpu.VMEM((ROWS, 128), F32),
             pltpu.SemaphoreType.DMA((3,)),
             pltpu.SemaphoreType.DMA((ITERS, 6)),
             pltpu.SemaphoreType.DMA((ITERS, 6)),
-            pltpu.SemaphoreType.DMA((3,)),
-            pltpu.SemaphoreType.DMA((3,)),
+            pltpu.SemaphoreType.DMA((5,)),
+            pltpu.SemaphoreType.DMA((5,)),
             pltpu.SemaphoreType.DMA((8,)),
             pltpu.SemaphoreType.DMA((8,)),
-            pltpu.SemaphoreType.DMA((2,)),
+            pltpu.SemaphoreType.DMA((1,)),
         ],
         compiler_params=pltpu.CompilerParams(
             collective_id=0, has_side_effects=True, vmem_limit_bytes=56 * 1024 * 1024
@@ -383,8 +426,15 @@
         cost_estimate=pl.CostEstimate(flops=500_000_000, bytes_accessed=4_000_000, transcendentals=0),
         name="smooth",
     )(right, hop_blocks[0], restriction[0])
+    x, coarse = pl.pallas_call(
+        hand_over,
+        out_shape=shapes,
+        in_specs=[pl.BlockSpec(memory_space=pltpu.VMEM)] * 2,
+        out_specs=(pl.BlockSpec(memory_space=pltpu.VMEM),) * 2,
+        name="hand_over",
+    )(*held)
     x = jnp.transpose(x.reshape(RHS, SITES, 128), (1, 0, 2))[None]
-    return x, jnp.transpose(coarse, (0, 2, 1, 3))
+    return x, jnp.transpose(coarse.reshape(8, RHS, 4, 128), (0, 2, 1, 3))
 
 
 def solution(mesh):

time: 77.3 us -> 73.6 us (0.952)
  local copies, waits for them, and re-layouts: 3.16 us -> 0 us
    unnamed x2 -> x0, local copies, waits for them, and re-layouts: 3.16 us -> none
    pallas_call x1 -> x2, Pallas kernels: 73.3 us -> 72.8 us  [the longest x1 71.1 us: per_device(): pl.pallas_call(body, out_shape=shapes, in_specs=[pl.BlockSpec(memory_spac...]
where the time goes in v2:
time: 73.6 us; the launch traced here: 73.4 us
  Pallas kernels  72.8 us (99%)
    pallas_call x1, Pallas kernels, per_device(): pl.pallas_call(body, out_shape=shapes, in_specs=[pl.BlockSpec(memory_spac...  71.1 us
    pallas_call x1, Pallas kernels, per_device(): pl.pallas_call(hand_over, out_shape=shapes, in_specs=[pl.BlockSpec(memory...  1.69 us

profile of v2, /device:TPU:1, one launch (start us, length us, event | category | flops | bytes accessed | tf_op | source)
XLA Modules:
  0.0 73.4 jit_solution(2010654710408574893)
XLA Ops:
  0.6 71.1 %smooth.1 = (f32[192,128]{1,0:T(8,128)}, f32[8,48,128]{2,1,0:T(8,128)}) custom-call(f32[192,128]{1,0:T(8,128)} %bitcast.17, bf16[16,9,64,128]{3,2,1,0:T(8,128)(2,1)} %bitcast.15, f32[16,64,128]{2,1,0:T(8,128)} %bitcast.16), custom_call_target="tpu_custom_call" | custom-call | flops 500000000 | bytes 4000000 | tf_op jit(solution)/shard_map/smooth/pallas_call | solution.py:388
  71.7 1.7 %hand_over.1 = (f32[192,128]{1,0:T(8,128)}, f32[8,48,128]{2,1,0:T(8,128)}) custom-call(f32[192,128]{1,0:T(8,128)} %get-tuple-element.6.x_in, f32[8,48,128]{2,1,0:T(8,128)} %get-tuple-element.7.coarse_in), custom_call_target="tpu_custom_call" | custom-call | tf_op jit(solution)/shard_map/hand_over/pallas_call | solution.py:429

commit v3 on v2

--- a/solution.py
+++ b/solution.py
@@ -21,6 +21,14 @@
     return lax.dot_general(lhs, rhs, (((1,), (1,)), ((), ())), preferred_element_type=F32)
 
 
+def mod(value, size):
+    return lax.rem(value, jnp.int32(size))
+
+
+def div(value, size):
+    return lax.div(value, jnp.int32(size))
+
+
 def split(value):
     high = value.astype(BF16)
     return high, (value - high.astype(F32)).astype(BF16)
@@ -45,15 +53,14 @@
 def body(
     right_ref, hop_ref, rest_ref, x_ref, coarse_ref,
     rin, hop, rest, vecs, sent, local, big, rows, acc, grams, message, slots0, slots1, slots2, wide_msg,
-    rest_hi, rest_lo, mine, posted, xout,
+    coarse, rest_hi, rest_lo, mine, posted, xout,
     load_sem, send_sem, recv_sem, red_send, red_recv, gat_send, gat_recv, out_sem,
 ):
     w = lax.axis_index("wide")
     n = lax.axis_index("narrow")
-    ylat, zlat = w % 8, w // 8
-    px, pz, plo = w % 8, (w // 8) % 8, w // 64
-    phi, pc = n // 2, n % 2
-    py = phi * 2 + plo
+    px, zlat = mod(w, 8), div(w, 8)
+    pz, plo = mod(zlat, 8), div(w, 64)
+    phi, pc = div(n, 2), mod(n, 2)
 
     load_right = pltpu.make_async_copy(right_ref, rin, load_sem.at[0])
     load_right.start()
@@ -62,30 +69,26 @@
     load_rest = pltpu.make_async_copy(rest_ref, rest, load_sem.at[2])
     load_rest.start()
 
-    z_up, z_down = (((zlat + 1) % 16) * 8 + ylat, n), (((zlat + 15) % 16) * 8 + ylat, n)
-    y_up, y_down = (zlat * 8 + (ylat + 1) % 8, n), (zlat * 8 + (ylat + 7) % 8, n)
-    t_up, t_down = (w, (n + 1) % 8), (w, (n + 7) % 8)
-
-    other = (w, phi * 2 + (1 - pc))
-
-    def at_xy(offset):
-        return ((w // 8) * 8 + (px + offset) % 8, ((phi + offset // 8) % 4) * 2 + pc)
-
-    def at_zy(offset):
-        return (((plo + offset // 8) % 2) * 64 + ((pz + offset) % 8) * 8 + px, n)
-
-    wide_steps = [1 + k + 15 * pc for k in range(16)]
-    deep_steps = [1 + k + 7 * pc for k in range(8)]
-
-    def back_xy(offset):
-        return ((w // 8) * 8 + (px + 64 - offset) % 8, ((phi + 4 - offset // 8) % 4) * 2 + pc)
-
-    def back_zy(offset):
-        return (((plo + 2 - offset // 8) % 2) * 64 + ((pz + 64 - offset) % 8) * 8 + px, n)
-
-    gathered = [(w, ((phi + k) % 4) * 2 + pc) for k in (2, 1, 3)]
-    greeted = [z_up, z_down, t_up, t_down, y_up, y_down, other] + gathered
-    greeted += [back_xy(o) for o in wide_steps] + [back_zy(o) for o in deep_steps]
+    in_x = [zlat * 8 + mod(px + d, 8) for d in range(8)]
+    in_z = [mod(pz + d, 8) * 8 + px for d in range(8)]
+    in_time = [mod(phi + d, 4) * 2 + pc for d in range(4)]
+
+    z_up, z_down = (mod(zlat + 1, 16) * 8 + px, n), (mod(zlat + 15, 16) * 8 + px, n)
+    y_up, y_down = (in_x[1], n), (in_x[7], n)
+    t_up, t_down = (w, mod(n + 1, 8)), (w, mod(n + 7, 8))
+    other = (w, n + 1 - 2 * pc)
+
+    ahead = [mod(phi + 2 * pc, 4) * 2 + pc, mod(phi + 2 * pc + 1, 4) * 2 + pc]
+    behind = [mod(phi + 4 - 2 * pc, 4) * 2 + pc, mod(phi + 3 - 2 * pc, 4) * 2 + pc]
+    wide_to = [(w, in_time[2])] + [(in_x[k % 8], ahead[k // 8]) for k in range(1, 16)]
+    wide_from = [(w, in_time[2])] + [(in_x[(8 - k) % 8], behind[k // 8]) for k in range(1, 16)]
+    half = mod(plo + pc, 2) * 64
+    deep_to = [(in_z[0] + 64 - 64 * plo, n)] + [(in_z[k] + half, n) for k in range(1, 8)]
+    deep_from = [deep_to[0]] + [(in_z[8 - k] + half, n) for k in range(1, 8)]
+
+    gathered = [(w, in_time[k]) for k in (2, 1, 3)]
+    greeted = [z_up, z_down, t_up, t_down, y_up, y_down, (w, mod(phi + 1 + 2 * pc, 4) * 2 + pc)]
+    greeted += wide_from + deep_from
     barrier = pltpu.get_barrier_semaphore()
     for device in greeted:
         pl.semaphore_signal(barrier, inc=1, device_id=device, device_id_type=MESH)
@@ -183,6 +186,12 @@
         def _():
             load_hop.wait()
 
+        @pl.when(i == 1)
+        def _():
+            load_rest.wait()
+            for site in range(SITES):
+                rest_hi[site], rest_lo[site] = split(rest[site])
+
         early(i)
         gram(i)
         for k in (4, 5, 0, 1):
@@ -219,33 +228,55 @@
         return [pltpu.make_async_copy(slots, slots, sem.at[phase]) for sem in (red_recv, red_send)]
 
     def part(own, slots):
-        return jnp.sum(slots[1:], 0) + jnp.where(pc == 0, own + slots[0], 0.0)
+        return jnp.sum(slots[1:], 0) + jnp.where(pc == 0, own, slots[0])
+
+    def restrict(j):
+        pieces = []
+        for h in range(2):
+            rows_of = [split(vecs[j, pl.ds(SLAB * y + PACK * h, PACK), :]) for y in range(2)]
+            both_rows = jnp.concatenate([paired(jnp.concatenate(p, 0)) for p in rows_of], 1)
+            high_rows = jnp.concatenate([paired(p[0]) for p in rows_of], 1)
+
+            def blocks(ref):
+                return jnp.concatenate([ref[8 * y + 4 * h : 8 * y + 4 * h + 4].reshape(256, 128) for y in range(2)], 1)
+
+            main = dot(both_rows, blocks(rest_hi))
+            remainder = dot(high_rows, blocks(rest_lo))
+            first = main[0:48] + main[48:96] + remainder[0:48]
+            second = main[96:144] + main[144:192] + remainder[48:96]
+            value = unpack(first, second)
+            value = value + pltpu.roll(value, PACK - RHS, 0)
+            pieces += [value[0:12], value[24:36]]
+        coarse[j] = jnp.concatenate(pieces, 0)
+
+    def restrict_some(start, stop):
+        def one(j, carry):
+            restrict(j)
+            return carry
+
+        lax.fori_loop(start, stop, one, 0)
 
     waits = [reduce_over(0, [other], slots0.at[0:1])]
-    load_rest.wait()
     waits[0][0].wait()
     message[1] = message[0] + slots0[0]
-    waits.append(reduce_over(1, [at_xy(o) for o in wide_steps], slots1))
-    for site in range(SITES):
-        rest_hi[site], rest_lo[site] = split(rest[site])
+    waits.append(reduce_over(1, wide_to, slots1))
+    restrict_some(0, 3)
     waits[1][0].wait()
     message[2] = part(message[1], slots1[...])
     waits.append(reduce_over(2, [other], slots0.at[1:2]))
     waits[2][0].wait()
     message[3] = message[2] + slots0[1]
-    waits.append(reduce_over(3, [at_zy(o) for o in deep_steps], slots2))
+    waits.append(reduce_over(3, deep_to, slots2))
 
     def drain(i, carry):
         for copy in halo(i):
             copy.wait_send()
         return carry
 
-    lax.fori_loop(0, ITERS, drain, 0)
+    restrict_some(3, 5)
     waits[3][0].wait()
     message[4] = part(message[3], slots2[...])
     waits.append(reduce_over(4, [other], slots0.at[2:3]))
-    for wait in waits[:4]:
-        wait[1].wait()
     waits[4][0].wait()
     total = message[4] + slots0[2]
     wide_msg[0:4, :] = total
@@ -314,38 +345,14 @@
         imag = spread(pair[1])
         return spread(pair[0])[None], jnp.where(left_half, -imag, imag)[None]
 
-    def vector(j):
-        return vecs[j].reshape(8, 24, 128), pltpu.roll(vecs[j], HALF, 1).reshape(8, 24, 128)
-
-    last = vecs[0].reshape(8, 24, 128)
-    field = jnp.zeros((8, 24, 128), F32)
-    for j in range(5):
-        plain, turned = vector(j)
-        if j > 0:
-            re, im = coefficient(residual[j])
-            last = last + re * plain + im * turned
-        if j < ITERS:
-            re, im = coefficient(iterate[j])
-            field = field + re * plain + im * turned
-    last = last.reshape(ROWS, 128)
-    field = field.reshape(ROWS, 128)
-
-    for h in range(2):
-        pieces = [split(last[SLAB * y + PACK * h : SLAB * y + PACK * (h + 1)]) for y in range(2)]
-        both_rows = jnp.concatenate([paired(jnp.concatenate(p, 0)) for p in pieces], 1)
-        high_rows = jnp.concatenate([paired(p[0]) for p in pieces], 1)
-
-        def blocks(ref):
-            return jnp.concatenate([ref[8 * y + 4 * h : 8 * y + 4 * h + 4].reshape(256, 128) for y in range(2)], 1)
-
-        main = dot(both_rows, blocks(rest_hi))
-        rest_part = dot(high_rows, blocks(rest_lo))
-        first = main[0:48] + main[48:96] + rest_part[0:48]
-        second = main[96:144] + main[144:192] + rest_part[48:96]
-        value = unpack(first, second)
-        value = value + pltpu.roll(value, PACK - RHS, 0)
-        mine[pl.ds(2 * h, RHS, stride=4), :] = value[0:12]
-        mine[pl.ds(2 * h + 1, RHS, stride=4), :] = value[24:36]
+    last = coarse[0].reshape(2, 24, 128)
+    for j in range(1, 5):
+        re, im = coefficient(residual[j])
+        last = last + re * coarse[j].reshape(2, 24, 128)
+        last = last + im * pltpu.roll(coarse[j], HALF, 1).reshape(2, 24, 128)
+    last = last.reshape(PACK, 128)
+    for at in range(4):
+        mine[pl.ds(at, RHS, stride=4), :] = last[RHS * at : RHS * (at + 1)]
     posted[n] = mine[...].astype(BF16)
 
     def gather(k, slot, device):
@@ -358,14 +365,23 @@
     first_hop.append(gather(0, n, other))
     for copy in first_hop:
         copy.start()
+    field = jnp.zeros((8, 24, 128), F32)
+    for j in range(ITERS):
+        re, im = coefficient(iterate[j])
+        field = field + re * vecs[j].reshape(8, 24, 128)
+        field = field + im * pltpu.roll(vecs[j], HALF, 1).reshape(8, 24, 128)
+    field = field.reshape(ROWS, 128)
     for site in range(SITES):
         xout[pl.ds(site, RHS, stride=SITES), :] = field[RHS * site : RHS * (site + 1)]
     put_x = pltpu.make_async_copy(xout, x_ref, out_sem.at[0])
     put_x.start()
+    lax.fori_loop(0, ITERS, drain, 0)
+    for wait in waits:
+        wait[1].wait()
     second_hop = []
     for k, copy in zip((1, 3, 2), (first_hop[1], first_hop[2], first_hop[0])):
         copy.wait_recv()
-        second_hop.append(gather(4 + k, ((phi + 4 - k) % 4) * 2 + pc, other))
+        second_hop.append(gather(4 + k, in_time[4 - k], other))
         second_hop[-1].start()
     first_hop[3].wait_recv()
     for copy in second_hop:
@@ -373,7 +389,6 @@
     coarse_ref[...] = posted[...].astype(F32)
     for copy in first_hop + second_hop:
         copy.wait_send()
-    waits[4][1].wait()
     put_x.wait()
 
 
@@ -406,6 +421,7 @@
             pltpu.VMEM((16, 4, 128), F32),
             pltpu.VMEM((8, 4, 128), F32),
             pltpu.VMEM((8, 128), F32),
+            pltpu.VMEM((ITERS + 1, PACK, 128), F32),
             pltpu.VMEM((SITES, 64, 128), BF16),
             pltpu.VMEM((SITES, 64, 128), BF16),
             pltpu.VMEM((4 * RHS, 128), F32),

time: 73.6 us -> 73 us (level)
  no operation moved by 1% of the time
where the time goes in v3:
time: 73 us; the launch traced here: 72.8 us
  Pallas kernels  72.2 us (99%)
    pallas_call x1, Pallas kernels, per_device(): pl.pallas_call(body, out_shape=shapes, in_specs=[pl.BlockSpec(memory_spac...  70.5 us
    pallas_call x1, Pallas kernels, per_device(): pl.pallas_call(hand_over, out_shape=shapes, in_specs=[pl.BlockSpec(memory...  1.69 us

profile of v3, /device:TPU:1, one launch (start us, length us, event | category | flops | bytes accessed | tf_op | source)
XLA Modules:
  0.0 72.8 jit_solution(6739150802422243672)
XLA Ops:
  0.6 70.5 %smooth.1 = (f32[192,128]{1,0:T(8,128)}, f32[8,48,128]{2,1,0:T(8,128)}) custom-call(f32[192,128]{1,0:T(8,128)} %bitcast.17, bf16[16,9,64,128]{3,2,1,0:T(8,128)(2,1)} %bitcast.15, f32[16,64,128]{2,1,0:T(8,128)} %bitcast.16), custom_call_target="tpu_custom_call" | custom-call | flops 500000000 | bytes 4000000 | tf_op jit(solution)/shard_map/smooth/pallas_call | solution.py:403
  71.1 1.7 %hand_over.1 = (f32[192,128]{1,0:T(8,128)}, f32[8,48,128]{2,1,0:T(8,128)}) custom-call(f32[192,128]{1,0:T(8,128)} %get-tuple-element.6.x_in, f32[8,48,128]{2,1,0:T(8,128)} %get-tuple-element.7.coarse_in), custom_call_target="tpu_custom_call" | custom-call | tf_op jit(solution)/shard_map/hand_over/pallas_call | solution.py:445

commit v4 on v3

--- a/solution.py
+++ b/solution.py
@@ -51,9 +51,9 @@
 
 
 def body(
-    right_ref, hop_ref, rest_ref, x_ref, coarse_ref,
+    right_ref, hop_ref, rest_ref, x_ref, posted,
     rin, hop, rest, vecs, sent, local, big, rows, acc, grams, message, slots0, slots1, slots2, wide_msg,
-    coarse, rest_hi, rest_lo, mine, posted, xout,
+    coarse, rest_hi, rest_lo, mine, xout,
     load_sem, send_sem, recv_sem, red_send, red_recv, gat_send, gat_recv, out_sem,
 ):
     w = lax.axis_index("wide")
@@ -386,7 +386,6 @@
     first_hop[3].wait_recv()
     for copy in second_hop:
         copy.wait_recv()
-    coarse_ref[...] = posted[...].astype(F32)
     for copy in first_hop + second_hop:
         copy.wait_send()
     put_x.wait()
@@ -394,15 +393,17 @@
 
 def hand_over(x_in, coarse_in, x_out, coarse_out):
     x_out[...] = x_in[...]
-    coarse_out[...] = coarse_in[...]
+    coarse_out[...] = coarse_in[...].astype(F32)
 
 
 def per_device(right_side, hop_blocks, restriction):
     right = jnp.transpose(right_side[0], (1, 0, 2)).reshape(ROWS, 128)
-    shapes = (jax.ShapeDtypeStruct((ROWS, 128), F32), jax.ShapeDtypeStruct((8, 4 * RHS, 128), F32))
+    def shapes(kind):
+        return (jax.ShapeDtypeStruct((ROWS, 128), F32), jax.ShapeDtypeStruct((8, 4 * RHS, 128), kind))
+
     held = pl.pallas_call(
         body,
-        out_shape=shapes,
+        out_shape=shapes(BF16),
         in_specs=[pl.BlockSpec(memory_space=pl.ANY)] * 3,
         out_specs=(pl.BlockSpec(memory_space=pl.ANY), pl.BlockSpec(memory_space=pltpu.VMEM)),
         scratch_shapes=[
@@ -425,7 +426,6 @@
             pltpu.VMEM((SITES, 64, 128), BF16),
             pltpu.VMEM((SITES, 64, 128), BF16),
             pltpu.VMEM((4 * RHS, 128), F32),
-            pltpu.VMEM((8, 4 * RHS, 128), BF16),
             pltpu.VMEM((ROWS, 128), F32),
             pltpu.SemaphoreType.DMA((3,)),
             pltpu.SemaphoreType.DMA((ITERS, 6)),
@@ -444,7 +444,7 @@
     )(right, hop_blocks[0], restriction[0])
     x, coarse = pl.pallas_call(
         hand_over,
-        out_shape=shapes,
+        out_shape=shapes(F32),
         in_specs=[pl.BlockSpec(memory_space=pltpu.VMEM)] * 2,
         out_specs=(pl.BlockSpec(memory_space=pltpu.VMEM),) * 2,
         name="hand_over",

time: 73 us -> 72.9 us (level)
  no operation moved by 1% of the time
where the time goes in v4:
time: 72.9 us; the launch traced here: 72.7 us
  Pallas kernels  72.1 us (99%)
    pallas_call x1, Pallas kernels, per_device(): pl.pallas_call(body, out_shape=shapes(BF16), in_specs=[pl.BlockSpec(memor...  70.4 us
    pallas_call x1, Pallas kernels, per_device(): pl.pallas_call(hand_over, out_shape=shapes(F32), in_specs=[pl.BlockSpec(m...  1.66 us

profile of v4, /device:TPU:1, one launch (start us, length us, event | category | flops | bytes accessed | tf_op | source)
XLA Modules:
  0.0 72.7 jit_solution(3435220389162601507)
XLA Ops:
  0.6 70.4 %smooth.1 = (f32[192,128]{1,0:T(8,128)}, bf16[8,48,128]{2,1,0:T(8,128)(2,1)}) custom-call(f32[192,128]{1,0:T(8,128)} %bitcast.17, bf16[16,9,64,128]{3,2,1,0:T(8,128)(2,1)} %bitcast.15, f32[16,64,128]{2,1,0:T(8,128)} %bitcast.16), custom_call_target="tpu_custom_call" | custom-call | flops 500000000 | bytes 4000000 | tf_op jit(solution)/shard_map/smooth/pallas_call | solution.py:404
  71.1 1.7 %hand_over.1 = (f32[192,128]{1,0:T(8,128)}, f32[8,48,128]{2,1,0:T(8,128)}) custom-call(f32[192,128]{1,0:T(8,128)} %get-tuple-element.6.x_in, bf16[8,48,128]{2,1,0:T(8,128)(2,1)} %get-tuple-element.7.coarse_in), custom_call_target="tpu_custom_call" | custom-call | tf_op jit(solution)/shard_map/hand_over/pallas_call | solution.py:445
